TPU v7x, 128 devices: a whole 4x4x4 slice. The times are simulated.
128 devices in a mesh: gx: 8 (over y, x_lo), gy: 8 (over x_hi, z), ga: 2 (over core).
Axes of the slice: x: 4 (x_hi: 2, x_lo: 2; x = x_hi * 2 + x_lo), y: 4, z: 4, core: 2. Of those that a mesh axis runs over, the one named last changes fastest.
Arguments:
- fields: float32 [5, 16, 128, 2048], P(None, 'ga', 'gx', 'gy'), may hold values from -6 to 6
- stiffness: float32 [16, 128, 2048], P('ga', 'gx', 'gy'), may hold values from 0.25 to 4
- lift_weight: float32 [5, 32], replicated, may hold values from -2.5 to 2.5
- lift_bias: float32 [32], replicated, may hold values from -3 to 3
- mix_weight: bfloat16 [32, 32], replicated, may hold values from -0.5 to 0.5
- spectral_weight: float32 [8, 32, 32, 32, 128], P('ga', 'gy', None, 'gx'), may hold values from -0.48 to 0.48
- output_bias: float32 [32], replicated, may hold values from -3 to 3
Outputs:
- layer_out: bfloat16 [16, 32, 64, 1024], P('ga', None, 'gx', 'gy')
All inputs are finite; a program needn't handle non-finite values.
Results may differ from a plain program's by a relative error of at most 0.01.
Values may be sent and summed in bfloat16 or wider, within the bound.
No kernel may reach another device: no remote copies, remote signals or barrier semaphores. Data moves between devices by JAX's collectives and lax.ppermute only.
A program may use at most 128 MiB of HBM per device.

v0:
```python
import math
import jax
import jax.numpy as jnp
from jax import lax
from jax.sharding import PartitionSpec as P

STEPS = 3
MX = 32
MY = 64
MZ = 8
courant_half = 0.1
smooth_half = 0.15
mean_flow = (0.3, -0.2, 0.1)
highest = lax.Precision.HIGHEST


def padded_2(block, sides, width):
    for axis, dim in sides:
        count = lax.axis_size(axis)
        forward = [(i, i + 1) for i in range(count - 1)]
        forward.append((count - 1, 0))
        backward = [(target, source) for source, target in forward]
        low = lax.ppermute(
            lax.slice_in_dim(block, block.shape[dim] - width, None, axis=dim), axis, forward
        )
        high = lax.ppermute(lax.slice_in_dim(block, 0, width, axis=dim), axis, backward)
        block = jnp.concatenate([low, block, high], axis=dim)
    return block


def step_interior(padded, stiff_part):
    center = padded[:, 1:-1, 1:-1, 1:-1]
    upper_depth = padded[:, 2:, 1:-1, 1:-1]
    lower_depth = padded[:, :-2, 1:-1, 1:-1]
    upper_east = padded[:, 1:-1, 2:, 1:-1]
    lower_east = padded[:, 1:-1, :-2, 1:-1]
    upper_north = padded[:, 1:-1, 1:-1, 2:]
    lower_north = padded[:, 1:-1, 1:-1, :-2]
    slope_depth = upper_depth - lower_depth
    slope_east = upper_east - lower_east
    slope_north = upper_north - lower_north
    curvature = (
        upper_depth
        + lower_depth
        + upper_east
        + lower_east
        + upper_north
        + lower_north
        - 6.0 * center
    )
    transport = mean_flow[0] * slope_east + mean_flow[1] * slope_north + mean_flow[2] * slope_depth
    diverge = slope_east[1] + slope_north[2] + slope_depth[3]
    coupling = jnp.stack(
        [diverge, slope_east[4], slope_north[4], slope_depth[4], stiff_part * diverge]
    )
    return center - courant_half * (transport + coupling) + smooth_half * curvature


def coarsen(fields_now):
    extent = fields_now.shape
    blocks = fields_now.reshape(extent[0], extent[1], extent[2] // 2, 2, extent[3] // 2, 2)
    return 0.25 * (
        blocks[:, :, :, 0, :, 0]
        + blocks[:, :, :, 1, :, 0]
        + blocks[:, :, :, 0, :, 1]
        + blocks[:, :, :, 1, :, 1]
    )


def angles(frequencies, points, length):
    product = jnp.mod(frequencies[:, None] * points[None, :], length)
    return product.astype(jnp.float32) * (2.0 * math.pi / length)


def centered(number):
    return jnp.arange(number, dtype=jnp.int32) - number // 2


def forward_east_table(points, length, mode_count):
    phases = angles(centered(mode_count), points, length)
    factor = 1.0 / math.sqrt(length)
    return (jnp.stack([jnp.cos(phases).T, -jnp.sin(phases).T], axis=1) * factor).astype(
        jnp.bfloat16
    )


def forward_north_table(points, length, mode_count):
    phases = angles(centered(mode_count), points, length)
    factor = 1.0 / math.sqrt(length)
    cosines = jnp.cos(phases).T * factor
    sines = jnp.sin(phases).T * factor
    return jnp.stack(
        [jnp.concatenate([cosines, -sines], axis=1), jnp.concatenate([sines, cosines], axis=1)],
        axis=0,
    )


def inverse_north_table(points, length, mode_count):
    phases = angles(centered(mode_count), points, length)
    factor = 1.0 / math.sqrt(length)
    cosines = jnp.cos(phases) * factor
    sines = jnp.sin(phases) * factor
    return jnp.concatenate(
        [jnp.stack([cosines, sines], axis=1), jnp.stack([-sines, cosines], axis=1)], axis=0
    )


def inverse_east_table(points, length, mode_count):
    phases = angles(centered(mode_count), points, length)
    factor = 1.0 / math.sqrt(length)
    return jnp.stack([jnp.cos(phases) * factor, -jnp.sin(phases) * factor], axis=1)


def forward_depth_blocks(values, points, frequencies, length):
    slot_count = frequencies.shape[0]
    phases = angles(frequencies.reshape(-1), points, length).reshape(
        slot_count, frequencies.shape[1], points.shape[0]
    )
    factor = 1.0 / math.sqrt(length)
    cosines = jnp.cos(phases) * factor
    sines = jnp.sin(phases) * factor
    halfway = values.shape[-1] // 2
    real_in = values[..., :halfway]
    imag_in = values[..., halfway:]
    real_part = jnp.einsum("zcrbn,rkz->rkcbn", real_in, cosines, precision=highest) + jnp.einsum(
        "zcrbn,rkz->rkcbn", imag_in, sines, precision=highest
    )
    imag_part = jnp.einsum("zcrbn,rkz->rkcbn", imag_in, cosines, precision=highest) - jnp.einsum(
        "zcrbn,rkz->rkcbn", real_in, sines, precision=highest
    )
    return jnp.concatenate([real_part, imag_part], axis=-1)


def mix_channels(coeffs, weight):
    halfway = coeffs.shape[-1] // 2
    real_in = coeffs[..., :halfway]
    imag_in = coeffs[..., halfway:]
    weight_real = weight[..., :halfway]
    weight_imag = weight[..., halfway:]
    real_part = jnp.einsum(
        "kcmn,kmcon->komn", real_in, weight_real, precision=highest
    ) - jnp.einsum("kcmn,kmcon->komn", imag_in, weight_imag, precision=highest)
    imag_part = jnp.einsum(
        "kcmn,kmcon->komn", imag_in, weight_real, precision=highest
    ) + jnp.einsum("kcmn,kmcon->komn", real_in, weight_imag, precision=highest)
    return jnp.concatenate([real_part, imag_part], axis=-1)


def inverse_depth(values, frequencies, points, length):
    phases = angles(frequencies, points, length)
    factor = 1.0 / math.sqrt(length)
    cosines = jnp.cos(phases) * factor
    sines = jnp.sin(phases) * factor
    halfway = values.shape[-1] // 2
    real_in = values[..., :halfway]
    imag_in = values[..., halfway:]
    real_part = jnp.einsum("komn,kz->zomn", real_in, cosines, precision=highest) - jnp.einsum(
        "komn,kz->zomn", imag_in, sines, precision=highest
    )
    imag_part = jnp.einsum("komn,kz->zomn", imag_in, cosines, precision=highest) + jnp.einsum(
        "komn,kz->zomn", real_in, sines, precision=highest
    )
    return jnp.concatenate([real_part, imag_part], axis=-1)


def shards(fields, stiffness, lift_weight, lift_bias, mix_weight, spectral_weight, output_bias):
    east_tiles = lax.axis_size("gx")
    north_tiles = lax.axis_size("gy")
    depth_groups = lax.axis_size("ga")
    fields_now = fields
    for repeat in range(STEPS):
        padded = padded_2(fields_now, (("gx", 2), ("gy", 3), ("ga", 1)), 1)
        fields_now = step_interior(padded, stiffness)
    filtered = coarsen(fields_now)
    pre_lift = (
        jnp.einsum("fzxy,fc->zcxy", filtered, lift_weight, precision=highest)
        + lift_bias[None, :, None, None]
    )
    lifted = jax.nn.gelu(pre_lift, approximate=True).astype(jnp.bfloat16)
    depth_local = lifted.shape[0]
    length_east = lifted.shape[2] * east_tiles
    length_north = lifted.shape[3] * north_tiles
    length_depth = depth_local * depth_groups
    east_points = jnp.arange(length_east, dtype=jnp.int32)
    north_points = jnp.arange(length_north, dtype=jnp.int32)
    table_east = forward_east_table(east_points, length_east, MX)
    table_north = forward_north_table(north_points, length_north, MY)
    planes = lax.all_to_all(
        lax.all_to_all(lifted, "gx", split_axis=1, concat_axis=2, tiled=True),
        "gy",
        split_axis=0,
        concat_axis=3,
        tiled=True,
    )
    east_modes = jnp.einsum(
        "zcxy,xpm->zcpmy", planes, table_east, preferred_element_type=jnp.float32
    )
    north_modes = jnp.einsum("zcpmy,pyq->zcmq", east_modes, table_north, precision=highest)
    plane_count = planes.shape[0]
    depth_points = (
        lax.axis_index("ga") * depth_local
        + lax.axis_index("gy") * plane_count
        + jnp.arange(plane_count, dtype=jnp.int32)
    )
    block_east = MX // north_tiles
    block_depth = MZ // depth_groups
    grouped = north_modes.reshape(
        plane_count, north_modes.shape[1], north_tiles, block_east, 2 * MY
    )
    owners = jnp.arange(1 * lax.axis_size(("gy", "ga")), dtype=jnp.int32)
    picked = jnp.take(grouped, owners // depth_groups, axis=2)
    frequencies = (owners % depth_groups)[:, None] * block_depth + jnp.arange(
        block_depth, dtype=jnp.int32
    )[None, :]
    coeffs = lax.psum_scatter(
        forward_depth_blocks(picked, depth_points, frequencies, length_depth).astype(jnp.bfloat16),
        ("gy", "ga"),
        scatter_dimension=0,
        tiled=True,
    ).astype(jnp.float32)[0]
    mixed_modes = mix_channels(lax.all_gather(coeffs, "gx", axis=1, tiled=True), spectral_weight)
    own_frequencies = lax.axis_index("ga") * coeffs.shape[0] + jnp.arange(
        coeffs.shape[0], dtype=jnp.int32
    )
    points = jnp.arange(depth_local * lax.axis_size("ga"), dtype=jnp.int32)
    back_depth = lax.psum_scatter(
        inverse_depth(mixed_modes, own_frequencies, points, length_depth),
        "ga",
        scatter_dimension=0,
        tiled=True,
    )
    back_north = jnp.einsum(
        "zomq,qpy->zompy",
        back_depth,
        inverse_north_table(north_points, length_north, MY),
        precision=highest,
    )
    all_modes = lax.all_to_all(back_north, "gy", split_axis=4, concat_axis=2, tiled=True)
    spectral = jnp.einsum(
        "zompy,mpx->zoxy",
        all_modes,
        inverse_east_table(east_points, length_east, MX),
        precision=highest,
    ).astype(jnp.bfloat16)
    spectral = lax.all_to_all(spectral, "gx", split_axis=2, concat_axis=1, tiled=True)
    direct = jnp.einsum("zcxy,co->zoxy", lifted, mix_weight, preferred_element_type=jnp.float32)
    summed = direct + output_bias[None, :, None, None] + spectral.astype(jnp.float32)
    return jax.nn.gelu(summed, approximate=True).astype(jnp.bfloat16)


def solution(mesh):
    placed = (
        P(None, "ga", "gx", "gy"),
        P("ga", "gx", "gy"),
        P(),
        P(),
        P(),
        P("ga", "gy", None, "gx", None),
        P(),
    )
    return jax.shard_map(
        shards, mesh=mesh, in_specs=placed, out_specs=P("ga", None, "gx", "gy"), check_vma=False
    )
```

profile of v0, /device:TPU:4, one launch (start us, length us, event | category | flops | bytes accessed | tf_op | source)
XLA Modules:
  0.0 481.4 jit_solution(12632177929340682965)
XLA Ops:
  6.5 1.2 fusion.133
  7.7 3.7 collective-permute-start
  11.5 1.7 collective-permute-done
  13.1 4.4 collective-permute-done.1
  17.6 1.2 pad_maximum_fusion
  19.0 4.3 collective-permute-start.2
  23.3 9.0 %collective-permute-done.2 = f32[5,8,18,1]{3,2,1,0:T(8,128)S(1)} collective-permute-done((f32[5,8,18,1]{3,2,1,0:T(8,128)S(1)}, f32[5,8,18,1]{3,2,1,0:T(8,128)S(1)}, u32[]{:S(2)}, u32[]{:S(2)}) %collective-permute-start.2) | collective-permute-done | bytes 2912 | tf_op jit(solution)/shard_map/ppermute | solution.py:26
  32.4 5.8 %collective-permute-done.3 = f32[5,8,18,1]{3,2,1,0:T(8,128)S(1)} collective-permute-done((f32[5,8,18,1]{3,2,1,0:T(8,128)S(1)}, f32[5,8,18,1]{3,2,1,0:T(8,128)S(1)}, u32[]{:S(2)}, u32[]{:S(2)}) %collective-permute-start.3) | collective-permute-done | bytes 2912 | tf_op jit(solution)/shard_map/ppermute | solution.py:23
  40.8 1.2 multiply_add_fusion.2
  43.0 1.1 collective-permute-start.7
  44.2 2.1 collective-permute-done.6
  46.3 2.8 collective-permute-done.7
  49.6 2.0 collective-permute-start.9
  51.6 9.9 %collective-permute-done.8 = f32[5,8,18,1]{3,2,1,0:T(8,128)S(1)} collective-permute-done((f32[5,8,18,1]{3,2,1,0:T(8,128)S(1)}, f32[5,8,18,1]{3,2,1,0:T(8,128)S(1)}, u32[]{:S(2)}, u32[]{:S(2)}) %collective-permute-start.8) | collective-permute-done | bytes 2912 | tf_op jit(solution)/shard_map/ppermute | solution.py:26
  61.5 3.7 collective-permute-done.9
  67.8 1.2 multiply_add_fusion.1
  69.4 1.7 collective-permute-start.13
  71.2 2.1 collective-permute-done.12
  73.3 2.2 collective-permute-done.13
  76.0 2.2 collective-permute-start.15
  78.1 9.8 %collective-permute-done.14 = f32[5,8,18,1]{3,2,1,0:T(8,128)S(1)} collective-permute-done((f32[5,8,18,1]{3,2,1,0:T(8,128)S(1)}, f32[5,8,18,1]{3,2,1,0:T(8,128)S(1)}, u32[]{:S(2)}, u32[]{:S(2)}) %collective-permute-start.14) | collective-permute-done | bytes 2912 | tf_op jit(solution)/shard_map/ppermute | solution.py:26
  88.0 3.9 collective-permute-done.15
  94.5 1.2 multiply_add_fusion
  95.6 5.5 %copy.39 = f32[5,8,16,256]{1,3,2,0:T(8,128)} copy(f32[5,8,16,256]{3,2,1,0:T(8,128)S(1)} %multiply_add_fusion) | data formatting | bytes 1310720 | tf_op jit(solution)/shard_map/add | solution.py:56
  101.1 10.9 %fusion = f32[5,8,8,1,128,1]{1,5,4,3,2,0:T(1,128)S(1)} fusion(f32[5,8,8,2,128,2]{1,5,4,3,2,0:T(2,128)} %bitcast.176), kind=kLoop, calls=%fused_computation.2 | loop fusion | flops 163840 | bytes 819200 | tf_op jit(solution)/shard_map/mul | solution.py:62
  112.1 1.1 copy.40
  113.2 1.3 fusion.13
  116.4 3.5 all-to-all-start
  119.9 2.1 fusion.47
  122.3 8.2 %all-to-all-done = bf16[8,32,8,128]{3,2,0,1:T(8,128)(2,1)S(1)} async-done(((bf16[8,32,8,128]{3,2,0,1:T(8,128)(2,1)}), bf16[8,32,8,128]{3,2,0,1:T(8,128)(2,1)S(1)}, u32[]{:S(2)}, u32[]{:S(2)}) %all-to-all-start) | async-done | bytes 524320 | tf_op jit(solution)/shard_map/all_to_all | solution.py:189
  131.5 5.9 %all-to-all-start.1 = ((bf16[8,4,64,128]{3,2,1,0:T(8,128)(2,1)}), bf16[8,4,64,128]{3,2,1,0:T(8,128)(2,1)S(1)}, u32[]{:S(2)}, u32[]{:S(2)}) async-start(bf16[8,4,64,128]{3,2,1,0:T(8,128)(2,1)} %bitcast.173), calls=%async_computation.1 | async-start | bytes 1048576 | tf_op jit(solution)/shard_map/all_to_all | solution.py:188
  137.9 8.0 %all-to-all-done.1 = bf16[8,4,64,128]{3,2,1,0:T(8,128)(2,1)S(1)} async-done(((bf16[8,4,64,128]{3,2,1,0:T(8,128)(2,1)}), bf16[8,4,64,128]{3,2,1,0:T(8,128)(2,1)S(1)}, u32[]{:S(2)}, u32[]{:S(2)}) %all-to-all-start.1) | async-done | bytes 524320 | tf_op jit(solution)/shard_map/all_to_all | solution.py:188
  147.1 1.6 convolution_bitcast_fusion.2
  151.8 134.7 %all-reduce.3.cloned.1.call-done = bf16[16,4,4,4,128]{4,3,2,1,0:T(4,128)(2,1)} async-done(((bf16[16,4,4,4,128]{4,3,2,1,0:T(4,128)(2,1)}), bf16[16,4,4,4,128]{4,3,2,1,0:T(4,128)(2,1)}) %all-reduce.3.cloned.1.call-update) | async-done | bytes 262160
  286.6 1.3 dynamic-slice_convert_fusion
  287.9 28.9 %all-gather = f32[1,4,32,4,128]{4,3,2,1,0:T(4,128)S(1)} all-gather(f32[1,4,4,4,128]{4,3,2,1,0:T(4,128)S(1)} %dynamic-slice_convert_fusion), channel_id=2, replica_groups=mesh['gx'=8,'gy'=8,'ga'=2] {'gx'}, dimensions={2}, use_global_device_ids=true | all-gather | bytes 294912 | tf_op jit(solution)/shard_map/all_gather | solution.py:221
  317.1 1.4 multiply_reduce_fusion.3
  321.3 1.1 sine_multiply_fusion.1
  322.4 7.2 %reduce-scatter.2.cloned.1.call-done = f32[8,4,4,128]{3,0,2,1:T(8,128)} async-done(((f32[16,4,4,128]{3,0,2,1:T(8,128)}), f32[8,4,4,128]{3,0,2,1:T(8,128)}) %reduce-scatter.2.cloned.1.call-update) | async-done | bytes 65552 | tf_op jit(solution)/shard_map/reduce_scatter | solution.py:226
  329.7 1.8 fusion.24
  331.5 17.0 %copy.48 = f32[8,4,4,2,1024]{0,3,2,1,4:T(2,128)} copy(f32[8,4,4,2,1024]{4,0,3,2,1:T(8,128)S(1)} %fusion.24) | data formatting | bytes 2097152 | tf_op jit(solution)/shard_map/zomq,qpy->zompy/dot_general | solution.py:232
  348.6 28.9 %reshape.560 = f32[8,1,32768]{2,1,0:T(1,128)} reshape(f32[1024,4,4,2,8]{4,3,2,1,0:T(2,128)} %bitcast.174) | data formatting | bytes 2097152
  377.5 7.8 %all-to-all-start.2 = ((f32[8,1,32768]{2,1,0:T(1,128)}), f32[8,1,32768]{2,1,0:T(1,128)S(1)}, u32[]{:S(2)}, u32[]{:S(2)}) async-start(f32[8,1,32768]{2,1,0:T(1,128)} %reshape.560), calls=%async_computation.3 | async-start | bytes 2097152 | tf_op jit(solution)/shard_map/all_to_all | solution.py:238
  385.4 14.2 %all-to-all-done.2 = f32[8,1,32768]{2,1,0:T(1,128)S(1)} async-done(((f32[8,1,32768]{2,1,0:T(1,128)}), f32[8,1,32768]{2,1,0:T(1,128)S(1)}, u32[]{:S(2)}, u32[]{:S(2)}) %all-to-all-start.2) | async-done | bytes 1048608 | tf_op jit(solution)/shard_map/all_to_all | solution.py:238
  400.1 3.3 reduce.8
  403.4 32.2 %reshape.561 = f32[1024,4,4,2,8]{4,3,2,1,0:T(2,128)} reshape(f32[8,32768]{1,0:T(8,128)S(1)} %reduce.8) | data formatting | bytes 2097152
  435.6 20.6 %copy.49 = f32[8,4,4,2,8,128]{5,2,4,3,1,0:T(4,128)S(1)} copy(f32[8,4,4,2,8,128]{0,3,2,1,5,4:T(2,128)} %bitcast.175) | data formatting | bytes 2097152 | tf_op jit(solution)/shard_map/all_to_all | solution.py:238
  457.7 14.7 %all_to_all.60 = bf16[8,4,64,128]{3,1,0,2:T(4,128)(2,1)S(1)} all-to-all(bf16[8,4,64,128]{3,1,0,2:T(4,128)(2,1)S(1)} %copy.50), channel_id=1, replica_groups=mesh['gx'=8,'gy'=8,'ga'=2] {'gx'}, dimensions={2} | all-to-all | bytes 1048576 | tf_op jit(solution)/shard_map/all_to_all | solution.py:245
  (111 shorter events, 24.8 us)
Async XLA Ops:
  6.5 466.1 %copy-start = (bf16[32,32]{1,0:T(8,128)(2,1)S(1)}, bf16[32,32]{1,0:T(8,128)(2,1)}, u32[]{:S(2)}) copy-start(bf16[32,32]{1,0:T(8,128)(2,1)} %param.11) | copy-start | bytes 6148
  6.5 31.7 %copy-start.1 = (f32[5,8,16,256]{3,2,1,0:T(8,128)S(1)}, f32[5,8,16,256]{3,2,1,0:T(8,128)}, u32[]{:S(2)}) copy-start(f32[5,8,16,256]{3,2,1,0:T(8,128)} %param.7) | copy-start | bytes 1966084
  7.7 5.4 %collective-permute-start = (f32[5,8,1,256]{3,2,1,0:T(1,128)S(1)}, f32[5,8,1,256]{3,2,1,0:T(1,128)S(1)}, u32[]{:S(2)}, u32[]{:S(2)}) collective-permute-start(f32[5,8,1,256]{3,2,1,0:T(1,128)S(1)} %get-tuple-element.34), channel_id=1, source_target_pairs={{16,0},{32,16},{48,32},{64,48},{80,64},{96,80},{112,96},{0,112},{1... | collective-permute-start | bytes 122888 | tf_op jit(solution)/shard_map/ppermute | solution.py:26
  11.5 6.1 %collective-permute-start.1 = (f32[5,8,1,256]{3,2,1,0:T(1,128)S(1)}, f32[5,8,1,256]{3,2,1,0:T(1,128)S(1)}, u32[]{:S(2)}, u32[]{:S(2)}) collective-permute-start(f32[5,8,1,256]{3,2,1,0:T(1,128)S(1)} %get-tuple-element.33), channel_id=1, source_target_pairs={{0,16},{16,32},{32,48},{48,64},{64,80},{80,96},{96,112},{112,0},{1... | collective-permute-start | bytes 122888 | tf_op jit(solution)/shard_map/ppermute | solution.py:23
  19.0 13.4 %collective-permute-start.2 = (f32[5,8,18,1]{3,2,1,0:T(8,128)S(1)}, f32[5,8,18,1]{3,2,1,0:T(8,128)S(1)}, u32[]{:S(2)}, u32[]{:S(2)}) collective-permute-start(f32[5,8,18,1]{3,2,1,0:T(8,128)S(1)} %get-tuple-element.22), channel_id=1, source_target_pairs={{2,0},{4,2},{6,4},{8,6},{10,8},{12,10},{14,12},{0,14},{3,1},{5,3},... | collective-permute-start | bytes 8648 | tf_op jit(solution)/shard_map/ppermute | solution.py:26
  23.3 14.9 %collective-permute-start.3 = (f32[5,8,18,1]{3,2,1,0:T(8,128)S(1)}, f32[5,8,18,1]{3,2,1,0:T(8,128)S(1)}, u32[]{:S(2)}, u32[]{:S(2)}) collective-permute-start(f32[5,8,18,1]{3,2,1,0:T(8,128)S(1)} %get-tuple-element.21), channel_id=1, source_target_pairs={{0,2},{2,4},{4,6},{6,8},{8,10},{10,12},{12,14},{14,0},{1,3},{3,5},... | collective-permute-start | bytes 8648 | tf_op jit(solution)/shard_map/ppermute | solution.py:23
  38.5 1.5 collective-permute-start.4
  38.6 1.7 collective-permute-start.5
  39.8 1.0 copy-start.3
  42.1 4.2 collective-permute-start.6
  43.0 6.1 %collective-permute-start.7 = (f32[5,8,1,256]{3,2,1,0:T(1,128)S(1)}, f32[5,8,1,256]{3,2,1,0:T(1,128)S(1)}, u32[]{:S(2)}, u32[]{:S(2)}) collective-permute-start(f32[5,8,1,256]{3,2,1,0:T(1,128)S(1)} %get-tuple-element.31), channel_id=1, source_target_pairs={{0,16},{16,32},{32,48},{48,64},{64,80},{80,96},{96,112},{112,0},{1... | collective-permute-start | bytes 122888 | tf_op jit(solution)/shard_map/ppermute | solution.py:23
  49.5 12.0 %collective-permute-start.8 = (f32[5,8,18,1]{3,2,1,0:T(8,128)S(1)}, f32[5,8,18,1]{3,2,1,0:T(8,128)S(1)}, u32[]{:S(2)}, u32[]{:S(2)}) collective-permute-start(f32[5,8,18,1]{3,2,1,0:T(8,128)S(1)} %get-tuple-element.20), channel_id=1, source_target_pairs={{2,0},{4,2},{6,4},{8,6},{10,8},{12,10},{14,12},{0,14},{3,1},{5,3},... | collective-permute-start | bytes 8648 | tf_op jit(solution)/shard_map/ppermute | solution.py:26
  49.6 15.6 %collective-permute-start.9 = (f32[5,8,18,1]{3,2,1,0:T(8,128)S(1)}, f32[5,8,18,1]{3,2,1,0:T(8,128)S(1)}, u32[]{:S(2)}, u32[]{:S(2)}) collective-permute-start(f32[5,8,18,1]{3,2,1,0:T(8,128)S(1)} %get-tuple-element.19), channel_id=1, source_target_pairs={{0,2},{2,4},{4,6},{6,8},{8,10},{10,12},{12,14},{14,0},{1,3},{3,5},... | collective-permute-start | bytes 8648 | tf_op jit(solution)/shard_map/ppermute | solution.py:23
  65.5 1.5 collective-permute-start.10
  65.6 1.7 collective-permute-start.11
  69.1 4.2 collective-permute-start.12
  69.4 6.1 %collective-permute-start.13 = (f32[5,8,1,256]{3,2,1,0:T(1,128)S(1)}, f32[5,8,1,256]{3,2,1,0:T(1,128)S(1)}, u32[]{:S(2)}, u32[]{:S(2)}) collective-permute-start(f32[5,8,1,256]{3,2,1,0:T(1,128)S(1)} %get-tuple-element.29), channel_id=1, source_target_pairs={{0,16},{16,32},{32,48},{48,64},{64,80},{80,96},{96,112},{112,0},{1... | collective-permute-start | bytes 122888 | tf_op jit(solution)/shard_map/ppermute | solution.py:23
  75.9 12.1 %collective-permute-start.14 = (f32[5,8,18,1]{3,2,1,0:T(8,128)S(1)}, f32[5,8,18,1]{3,2,1,0:T(8,128)S(1)}, u32[]{:S(2)}, u32[]{:S(2)}) collective-permute-start(f32[5,8,18,1]{3,2,1,0:T(8,128)S(1)} %get-tuple-element.18), channel_id=1, source_target_pairs={{2,0},{4,2},{6,4},{8,6},{10,8},{12,10},{14,12},{0,14},{3,1},{5,3},... | collective-permute-start | bytes 8648 | tf_op jit(solution)/shard_map/ppermute | solution.py:26
  76.0 15.9 %collective-permute-start.15 = (f32[5,8,18,1]{3,2,1,0:T(8,128)S(1)}, f32[5,8,18,1]{3,2,1,0:T(8,128)S(1)}, u32[]{:S(2)}, u32[]{:S(2)}) collective-permute-start(f32[5,8,18,1]{3,2,1,0:T(8,128)S(1)} %get-tuple-element.17), channel_id=1, source_target_pairs={{0,2},{2,4},{4,6},{6,8},{8,10},{10,12},{12,14},{14,0},{1,3},{3,5},... | collective-permute-start | bytes 8648 | tf_op jit(solution)/shard_map/ppermute | solution.py:23
  92.1 1.5 collective-permute-start.16
  92.2 1.7 collective-permute-start.17
  112.0 1.2 copy-start.6
  112.1 1.2 copy-start.7
  114.6 0.8 copy-start.4
  116.4 14.2 %all-to-all-start = ((bf16[8,32,8,128]{3,2,0,1:T(8,128)(2,1)}), bf16[8,32,8,128]{3,2,0,1:T(8,128)(2,1)S(1)}, u32[]{:S(2)}, u32[]{:S(2)}) async-start(bf16[8,32,8,128]{3,2,0,1:T(8,128)(2,1)} %copy.42), calls=%async_computation | async-start | bytes 1048576 | tf_op jit(solution)/shard_map/all_to_all | solution.py:189
  131.5 14.4 %all-to-all-start.1 = ((bf16[8,4,64,128]{3,2,1,0:T(8,128)(2,1)}), bf16[8,4,64,128]{3,2,1,0:T(8,128)(2,1)S(1)}, u32[]{:S(2)}, u32[]{:S(2)}) async-start(bf16[8,4,64,128]{3,2,1,0:T(8,128)(2,1)} %bitcast.173), calls=%async_computation.1 | async-start | bytes 1048576 | tf_op jit(solution)/shard_map/all_to_all | solution.py:188
  137.4 149.2 %all-reduce.3.cloned.1.call-start = ((), (), s32[]{:S(2)}) async-start(), calls=%async_computation.6 | async-start | bytes 524288
  147.1 4.1 copy-start.9
  149.4 167.7 %copy-start.2 = (f32[4,4,32,4,128]{4,3,2,1,0:T(4,128)S(1)}, f32[4,4,32,4,128]{4,3,2,1,0:T(4,128)}, u32[]{:S(2)}) copy-start(f32[4,4,32,4,128]{4,3,2,1,0:T(4,128)} %param.12) | copy-start | bytes 3145732
  151.1 178.5 %reduce-scatter.2.cloned.1.call-start = ((), (), s32[]{:S(2)}) async-start(), calls=%async_computation.5 | async-start | bytes 196608 | tf_op jit(solution)/shard_map/reduce_scatter | solution.py:226
  377.5 22.1 %all-to-all-start.2 = ((f32[8,1,32768]{2,1,0:T(1,128)}), f32[8,1,32768]{2,1,0:T(1,128)S(1)}, u32[]{:S(2)}, u32[]{:S(2)}) async-start(f32[8,1,32768]{2,1,0:T(1,128)} %reshape.560), calls=%async_computation.3 | async-start | bytes 2097152 | tf_op jit(solution)/shard_map/all_to_all | solution.py:238
  456.2 16.5 %copy-start.5 = (bf16[8,32,8,128]{3,1,2,0:T(8,128)(2,1)S(1)}, bf16[8,32,8,128]{3,1,2,0:T(8,128)(2,1)}, u32[]{:S(2)}) copy-start(bf16[8,32,8,128]{3,1,2,0:T(8,128)(2,1)} %copy-done.4) | copy-start | bytes 1572868
  456.2 16.5 %copy-start.8 = (f32[32]{0:T(128)S(1)}, f32[32]{0:T(128)}, u32[]{:S(2)}) copy-start(f32[32]{0:T(128)} %param.13) | copy-start | bytes 388
Sparse Core Ops, SparseCore 0:
  151.2 135.2 all-reduce.2
  321.4 8.2 reduce-scatter.1
where the time goes:
time: 491 us; the launch traced here: 481 us
  waiting for transfers between devices  232 us (47%)
  local copies, waits for them, and re-layouts  115 us (23%)
  blocking collectives  43.6 us (9%)
  starting transfers between devices  35.7 us (7%)
  other arithmetic  32.6 us (7%)
  between operations  14.2 us (3%)
  matrix products  8.66 us (2%)
    unnamed x3, waiting for transfers between devices  135 us
    unnamed x35, local copies, waits for them, and re-layouts  63 us
    ppermute x9, waiting for transfers between devices, padded_2(): lax.ppermute(lax.slice_in_dim(block, 0, width, axis=dim), axis, backward)  35.4 us
    all_gather x1, blocking collectives, shards(): lax.all_gather(coeffs, 'gx', axis=1, tiled=True)  28.9 us
    ppermute x9, waiting for transfers between devices, padded_2(): lax.ppermute(lax.slice_in_dim(block, block.shape[dim] - width, None, axis...  23.7 us
    all_to_all x2, local copies, waits for them, and re-layouts, shards(): lax.all_to_all(back_north, 'gy', split_axis=4, concat_axis=2, tiled=True)  21.1 us
    dot_general x1, local copies, waits for them, and re-layouts, shards(): jnp.einsum('zomq,qpy->zompy', back_depth, inverse_north_table(north_point...  17 us
    all_to_all x1, blocking collectives, shards(): lax.all_to_all(spectral, 'gx', split_axis=2, concat_axis=1, tiled=True)  14.7 us
  transfers between devices with their start and end apart: 23, of which 23 were waited for; matrix products, arithmetic and copies ran while one was open for 1% of the time, Pallas kernels for 0%

commit v1 on v0

--- a/solution.py
+++ b/solution.py
@@ -12,6 +12,11 @@
 smooth_half = 0.15
 mean_flow = (0.3, -0.2, 0.1)
 highest = lax.Precision.HIGHEST
+
+
+def swapped_in(x, axis, along):
+    repeated = jnp.stack([x] * lax.axis_size(axis))
+    return jnp.concatenate(lax.all_to_all(repeated, axis, 0, 0), axis=along)
 
 
 def padded_2(block, sides, width):
@@ -218,7 +223,7 @@
         scatter_dimension=0,
         tiled=True,
     ).astype(jnp.float32)[0]
-    mixed_modes = mix_channels(lax.all_gather(coeffs, "gx", axis=1, tiled=True), spectral_weight)
+    mixed_modes = mix_channels(swapped_in(coeffs, "gx", 1), spectral_weight)
     own_frequencies = lax.axis_index("ga") * coeffs.shape[0] + jnp.arange(
         coeffs.shape[0], dtype=jnp.int32
     )

time: 491 us -> 475 us (0.967)
  blocking collectives: 43.6 us -> 14.7 us
  waiting for transfers between devices: 232 us -> 239 us
    all_gather x1 -> x0, blocking collectives: 28.9 us -> none  [shards(): lax.all_gather(coeffs, 'gx', axis=1, tiled=True)]
    all_to_all x0 -> x1, waiting for transfers between devices: none -> 7.22 us  [swapped_in(): return jnp.concatenate(lax.all_to_all(repeated, axis, 0, 0), axis=along)]
    unnamed x35 -> x33, local copies, waits for them, and re-layouts: 63 us -> 62.9 us
  transfers between devices with their start and end apart: 23 -> 24, of which waited for: 23 -> 24; matrix products, arithmetic and copies ran while one was open for 1% -> 1% of each run, Pallas kernels for 0% -> 0%
where the time goes in v1:
time: 475 us; the launch traced here: 466 us
  waiting for transfers between devices  239 us (50%)
  local copies, waits for them, and re-layouts  116 us (24%)
  starting transfers between devices  40.6 us (9%)
  other arithmetic  32.7 us (7%)
  blocking collectives  14.7 us (3%)
  between operations  14.3 us (3%)
  matrix products  8.68 us (2%)
    unnamed x3, waiting for transfers between devices  135 us
    unnamed x33, local copies, waits for them, and re-layouts  62.9 us
    ppermute x9, waiting for transfers between devices, padded_2(): lax.ppermute(lax.slice_in_dim(block, 0, width, axis=dim), axis, backward)  35.4 us
    ppermute x9, waiting for transfers between devices, padded_2(): lax.ppermute(lax.slice_in_dim(block, block.shape[dim] - width, None, axis...  23.7 us
    all_to_all x2, local copies, waits for them, and re-layouts, shards(): lax.all_to_all(back_north, 'gy', split_axis=4, concat_axis=2, tiled=True)  21.1 us
    dot_general x1, local copies, waits for them, and re-layouts, shards(): jnp.einsum('zomq,qpy->zompy', back_depth, inverse_north_table(north_point...  17 us
    all_to_all x1, blocking collectives, shards(): lax.all_to_all(spectral, 'gx', split_axis=2, concat_axis=1, tiled=True)  14.7 us
    all_to_all x1, waiting for transfers between devices, shards(): lax.all_to_all(back_north, 'gy', split_axis=4, concat_axis=2, tiled=True)  14.2 us
  transfers between devices with their start and end apart: 24, of which 24 were waited for; matrix products, arithmetic and copies ran while one was open for 1% of the time, Pallas kernels for 0%

profile of v1, /device:TPU:4, one launch (start us, length us, event | category | flops | bytes accessed | tf_op | source)
XLA Modules:
  0.0 465.8 jit_solution(4253091089648335298)
XLA Ops:
  6.5 1.2 fusion.133
  7.7 3.7 collective-permute-start
  11.5 1.7 collective-permute-done
  13.1 4.4 collective-permute-done.1
  17.6 1.2 pad_maximum_fusion
  19.0 4.3 collective-permute-start.2
  23.3 9.0 %collective-permute-done.2 = f32[5,8,18,1]{3,2,1,0:T(8,128)S(1)} collective-permute-done((f32[5,8,18,1]{3,2,1,0:T(8,128)S(1)}, f32[5,8,18,1]{3,2,1,0:T(8,128)S(1)}, u32[]{:S(2)}, u32[]{:S(2)}) %collective-permute-start.2) | collective-permute-done | bytes 2912 | tf_op jit(solution)/shard_map/ppermute | solution.py:31
  32.4 5.8 %collective-permute-done.3 = f32[5,8,18,1]{3,2,1,0:T(8,128)S(1)} collective-permute-done((f32[5,8,18,1]{3,2,1,0:T(8,128)S(1)}, f32[5,8,18,1]{3,2,1,0:T(8,128)S(1)}, u32[]{:S(2)}, u32[]{:S(2)}) %collective-permute-start.3) | collective-permute-done | bytes 2912 | tf_op jit(solution)/shard_map/ppermute | solution.py:28
  40.8 1.2 multiply_add_fusion.2
  43.0 1.1 collective-permute-start.7
  44.2 2.1 collective-permute-done.6
  46.3 2.8 collective-permute-done.7
  49.6 2.0 collective-permute-start.9
  51.6 9.9 %collective-permute-done.8 = f32[5,8,18,1]{3,2,1,0:T(8,128)S(1)} collective-permute-done((f32[5,8,18,1]{3,2,1,0:T(8,128)S(1)}, f32[5,8,18,1]{3,2,1,0:T(8,128)S(1)}, u32[]{:S(2)}, u32[]{:S(2)}) %collective-permute-start.8) | collective-permute-done | bytes 2912 | tf_op jit(solution)/shard_map/ppermute | solution.py:31
  61.5 3.7 collective-permute-done.9
  67.8 1.2 multiply_add_fusion.1
  69.4 1.7 collective-permute-start.13
  71.2 2.1 collective-permute-done.12
  73.3 2.2 collective-permute-done.13
  76.0 2.2 collective-permute-start.15
  78.1 9.8 %collective-permute-done.14 = f32[5,8,18,1]{3,2,1,0:T(8,128)S(1)} collective-permute-done((f32[5,8,18,1]{3,2,1,0:T(8,128)S(1)}, f32[5,8,18,1]{3,2,1,0:T(8,128)S(1)}, u32[]{:S(2)}, u32[]{:S(2)}) %collective-permute-start.14) | collective-permute-done | bytes 2912 | tf_op jit(solution)/shard_map/ppermute | solution.py:31
  88.0 3.9 collective-permute-done.15
  94.5 1.2 multiply_add_fusion
  95.6 5.4 %copy.44 = f32[5,8,16,256]{1,3,2,0:T(8,128)} copy(f32[5,8,16,256]{3,2,1,0:T(8,128)S(1)} %multiply_add_fusion) | data formatting | bytes 1310720 | tf_op jit(solution)/shard_map/add | solution.py:61
  101.1 10.9 %fusion = f32[5,8,8,1,128,1]{1,5,4,3,2,0:T(1,128)S(1)} fusion(f32[5,8,8,2,128,2]{1,5,4,3,2,0:T(2,128)} %bitcast.180), kind=kLoop, calls=%fused_computation.2 | loop fusion | flops 163840 | bytes 819200 | tf_op jit(solution)/shard_map/mul | solution.py:67
  112.0 1.1 copy.45
  113.1 1.3 fusion.13
  116.3 3.5 all-to-all-start
  119.8 2.1 fusion.47
  122.2 8.2 %all-to-all-done = bf16[8,32,8,128]{3,2,0,1:T(8,128)(2,1)S(1)} async-done(((bf16[8,32,8,128]{3,2,0,1:T(8,128)(2,1)}), bf16[8,32,8,128]{3,2,0,1:T(8,128)(2,1)S(1)}, u32[]{:S(2)}, u32[]{:S(2)}) %all-to-all-start) | async-done | bytes 524320 | tf_op jit(solution)/shard_map/all_to_all | solution.py:194
  131.4 5.9 %all-to-all-start.1 = ((bf16[8,4,64,128]{3,2,1,0:T(8,128)(2,1)}), bf16[8,4,64,128]{3,2,1,0:T(8,128)(2,1)S(1)}, u32[]{:S(2)}, u32[]{:S(2)}) async-start(bf16[8,4,64,128]{3,2,1,0:T(8,128)(2,1)} %bitcast.177), calls=%async_computation.1 | async-start | bytes 1048576 | tf_op jit(solution)/shard_map/all_to_all | solution.py:193
  137.8 8.0 %all-to-all-done.1 = bf16[8,4,64,128]{3,2,1,0:T(8,128)(2,1)S(1)} async-done(((bf16[8,4,64,128]{3,2,1,0:T(8,128)(2,1)}), bf16[8,4,64,128]{3,2,1,0:T(8,128)(2,1)S(1)}, u32[]{:S(2)}, u32[]{:S(2)}) %all-to-all-start.1) | async-done | bytes 524320 | tf_op jit(solution)/shard_map/all_to_all | solution.py:193
  147.0 1.6 convolution_bitcast_fusion.2
  151.8 135.0 %all-reduce.3.cloned.1.call-done = bf16[16,4,4,4,128]{4,2,3,1,0:T(4,128)(2,1)} async-done(((bf16[16,4,4,4,128]{4,2,3,1,0:T(4,128)(2,1)}), bf16[16,4,4,4,128]{4,2,3,1,0:T(4,128)(2,1)}) %all-reduce.3.cloned.1.call-update) | async-done | bytes 262160
  286.8 1.4 bitcast_convert_fusion
  288.9 4.9 %all-to-all-start.2 = ((f32[8,4,4,4,128]{4,2,3,1,0:T(4,128)}), f32[8,4,4,4,128]{4,2,3,1,0:T(4,128)S(1)}, u32[]{:S(2)}, u32[]{:S(2)}) async-start(f32[8,4,4,4,128]{4,2,3,1,0:T(4,128)} %stack.64), calls=%async_computation.2 | async-start | bytes 524288 | tf_op jit(solution)/shard_map/all_to_all | solution.py:19
  293.9 7.2 %all-to-all-done.2 = f32[8,4,4,4,128]{4,2,3,1,0:T(4,128)S(1)} async-done(((f32[8,4,4,4,128]{4,2,3,1,0:T(4,128)}), f32[8,4,4,4,128]{4,2,3,1,0:T(4,128)S(1)}, u32[]{:S(2)}, u32[]{:S(2)}) %all-to-all-start.2) | async-done | bytes 262176 | tf_op jit(solution)/shard_map/all_to_all | solution.py:19
  301.3 1.4 multiply_reduce_fusion.3
  306.6 7.5 %reduce-scatter.2.cloned.1.call-done = f32[8,4,4,128]{3,0,2,1:T(8,128)} async-done(((f32[16,4,4,128]{3,0,2,1:T(8,128)}), f32[8,4,4,128]{3,0,2,1:T(8,128)}) %reduce-scatter.2.cloned.1.call-update) | async-done | bytes 65552 | tf_op jit(solution)/shard_map/reduce_scatter | solution.py:231
  314.1 1.8 fusion.24
  316.0 17.0 %copy.56 = f32[8,4,4,2,1024]{0,3,2,1,4:T(2,128)} copy(f32[8,4,4,2,1024]{4,0,3,2,1:T(8,128)S(1)} %fusion.24) | data formatting | bytes 2097152 | tf_op jit(solution)/shard_map/zomq,qpy->zompy/dot_general | solution.py:237
  333.0 29.0 %reshape.569 = f32[8,1,32768]{2,1,0:T(1,128)} reshape(f32[1024,4,4,2,8]{4,3,2,1,0:T(2,128)} %bitcast.178) | data formatting | bytes 2097152
  362.0 7.8 %all-to-all-start.3 = ((f32[8,1,32768]{2,1,0:T(1,128)}), f32[8,1,32768]{2,1,0:T(1,128)S(1)}, u32[]{:S(2)}, u32[]{:S(2)}) async-start(f32[8,1,32768]{2,1,0:T(1,128)} %reshape.569), calls=%async_computation.4 | async-start | bytes 2097152 | tf_op jit(solution)/shard_map/all_to_all | solution.py:243
  369.9 14.2 %all-to-all-done.3 = f32[8,1,32768]{2,1,0:T(1,128)S(1)} async-done(((f32[8,1,32768]{2,1,0:T(1,128)}), f32[8,1,32768]{2,1,0:T(1,128)S(1)}, u32[]{:S(2)}, u32[]{:S(2)}) %all-to-all-start.3) | async-done | bytes 1048608 | tf_op jit(solution)/shard_map/all_to_all | solution.py:243
  384.6 3.3 reduce.8
  387.8 32.2 %reshape.570 = f32[1024,4,4,2,8]{4,3,2,1,0:T(2,128)} reshape(f32[8,32768]{1,0:T(8,128)S(1)} %reduce.8) | data formatting | bytes 2097152
  420.1 20.6 %copy.57 = f32[8,4,4,2,8,128]{5,2,4,3,1,0:T(4,128)S(1)} copy(f32[8,4,4,2,8,128]{0,3,2,1,5,4:T(2,128)} %bitcast.179) | data formatting | bytes 2097152 | tf_op jit(solution)/shard_map/all_to_all | solution.py:243
  442.1 14.7 %all_to_all.65 = bf16[8,4,64,128]{3,1,0,2:T(4,128)(2,1)S(1)} all-to-all(bf16[8,4,64,128]{3,1,0,2:T(4,128)(2,1)S(1)} %copy.58), channel_id=1, replica_groups=mesh['gx'=8,'gy'=8,'ga'=2] {'gx'}, dimensions={2} | all-to-all | bytes 1048576 | tf_op jit(solution)/shard_map/all_to_all | solution.py:250
  (114 shorter events, 26.7 us)
Async XLA Ops:
  6.5 450.6 %copy-start = (bf16[32,32]{1,0:T(8,128)(2,1)S(1)}, bf16[32,32]{1,0:T(8,128)(2,1)}, u32[]{:S(2)}) copy-start(bf16[32,32]{1,0:T(8,128)(2,1)} %param.11) | copy-start | bytes 6148
  6.5 31.7 %copy-start.1 = (f32[5,8,16,256]{3,2,1,0:T(8,128)S(1)}, f32[5,8,16,256]{3,2,1,0:T(8,128)}, u32[]{:S(2)}) copy-start(f32[5,8,16,256]{3,2,1,0:T(8,128)} %param.7) | copy-start | bytes 1966084
  7.7 5.4 %collective-permute-start = (f32[5,8,1,256]{3,2,1,0:T(1,128)S(1)}, f32[5,8,1,256]{3,2,1,0:T(1,128)S(1)}, u32[]{:S(2)}, u32[]{:S(2)}) collective-permute-start(f32[5,8,1,256]{3,2,1,0:T(1,128)S(1)} %get-tuple-element.34), channel_id=1, source_target_pairs={{16,0},{32,16},{48,32},{64,48},{80,64},{96,80},{112,96},{0,112},{1... | collective-permute-start | bytes 122888 | tf_op jit(solution)/shard_map/ppermute | solution.py:31
  11.5 6.1 %collective-permute-start.1 = (f32[5,8,1,256]{3,2,1,0:T(1,128)S(1)}, f32[5,8,1,256]{3,2,1,0:T(1,128)S(1)}, u32[]{:S(2)}, u32[]{:S(2)}) collective-permute-start(f32[5,8,1,256]{3,2,1,0:T(1,128)S(1)} %get-tuple-element.33), channel_id=1, source_target_pairs={{0,16},{16,32},{32,48},{48,64},{64,80},{80,96},{96,112},{112,0},{1... | collective-permute-start | bytes 122888 | tf_op jit(solution)/shard_map/ppermute | solution.py:28
  19.0 13.4 %collective-permute-start.2 = (f32[5,8,18,1]{3,2,1,0:T(8,128)S(1)}, f32[5,8,18,1]{3,2,1,0:T(8,128)S(1)}, u32[]{:S(2)}, u32[]{:S(2)}) collective-permute-start(f32[5,8,18,1]{3,2,1,0:T(8,128)S(1)} %get-tuple-element.22), channel_id=1, source_target_pairs={{2,0},{4,2},{6,4},{8,6},{10,8},{12,10},{14,12},{0,14},{3,1},{5,3},... | collective-permute-start | bytes 8648 | tf_op jit(solution)/shard_map/ppermute | solution.py:31
  23.3 14.9 %collective-permute-start.3 = (f32[5,8,18,1]{3,2,1,0:T(8,128)S(1)}, f32[5,8,18,1]{3,2,1,0:T(8,128)S(1)}, u32[]{:S(2)}, u32[]{:S(2)}) collective-permute-start(f32[5,8,18,1]{3,2,1,0:T(8,128)S(1)} %get-tuple-element.21), channel_id=1, source_target_pairs={{0,2},{2,4},{4,6},{6,8},{8,10},{10,12},{12,14},{14,0},{1,3},{3,5},... | collective-permute-start | bytes 8648 | tf_op jit(solution)/shard_map/ppermute | solution.py:28
  38.5 1.5 collective-permute-start.4
  38.6 1.7 collective-permute-start.5
  39.8 1.0 copy-start.3
  42.1 4.2 collective-permute-start.6
  43.0 6.1 %collective-permute-start.7 = (f32[5,8,1,256]{3,2,1,0:T(1,128)S(1)}, f32[5,8,1,256]{3,2,1,0:T(1,128)S(1)}, u32[]{:S(2)}, u32[]{:S(2)}) collective-permute-start(f32[5,8,1,256]{3,2,1,0:T(1,128)S(1)} %get-tuple-element.31), channel_id=1, source_target_pairs={{0,16},{16,32},{32,48},{48,64},{64,80},{80,96},{96,112},{112,0},{1... | collective-permute-start | bytes 122888 | tf_op jit(solution)/shard_map/ppermute | solution.py:28
  49.5 12.0 %collective-permute-start.8 = (f32[5,8,18,1]{3,2,1,0:T(8,128)S(1)}, f32[5,8,18,1]{3,2,1,0:T(8,128)S(1)}, u32[]{:S(2)}, u32[]{:S(2)}) collective-permute-start(f32[5,8,18,1]{3,2,1,0:T(8,128)S(1)} %get-tuple-element.20), channel_id=1, source_target_pairs={{2,0},{4,2},{6,4},{8,6},{10,8},{12,10},{14,12},{0,14},{3,1},{5,3},... | collective-permute-start | bytes 8648 | tf_op jit(solution)/shard_map/ppermute | solution.py:31
  49.6 15.6 %collective-permute-start.9 = (f32[5,8,18,1]{3,2,1,0:T(8,128)S(1)}, f32[5,8,18,1]{3,2,1,0:T(8,128)S(1)}, u32[]{:S(2)}, u32[]{:S(2)}) collective-permute-start(f32[5,8,18,1]{3,2,1,0:T(8,128)S(1)} %get-tuple-element.19), channel_id=1, source_target_pairs={{0,2},{2,4},{4,6},{6,8},{8,10},{10,12},{12,14},{14,0},{1,3},{3,5},... | collective-permute-start | bytes 8648 | tf_op jit(solution)/shard_map/ppermute | solution.py:28
  65.5 1.5 collective-permute-start.10
  65.6 1.7 collective-permute-start.11
  69.1 4.2 collective-permute-start.12
  69.4 6.1 %collective-permute-start.13 = (f32[5,8,1,256]{3,2,1,0:T(1,128)S(1)}, f32[5,8,1,256]{3,2,1,0:T(1,128)S(1)}, u32[]{:S(2)}, u32[]{:S(2)}) collective-permute-start(f32[5,8,1,256]{3,2,1,0:T(1,128)S(1)} %get-tuple-element.29), channel_id=1, source_target_pairs={{0,16},{16,32},{32,48},{48,64},{64,80},{80,96},{96,112},{112,0},{1... | collective-permute-start | bytes 122888 | tf_op jit(solution)/shard_map/ppermute | solution.py:28
  75.9 12.1 %collective-permute-start.14 = (f32[5,8,18,1]{3,2,1,0:T(8,128)S(1)}, f32[5,8,18,1]{3,2,1,0:T(8,128)S(1)}, u32[]{:S(2)}, u32[]{:S(2)}) collective-permute-start(f32[5,8,18,1]{3,2,1,0:T(8,128)S(1)} %get-tuple-element.18), channel_id=1, source_target_pairs={{2,0},{4,2},{6,4},{8,6},{10,8},{12,10},{14,12},{0,14},{3,1},{5,3},... | collective-permute-start | bytes 8648 | tf_op jit(solution)/shard_map/ppermute | solution.py:31
  76.0 15.9 %collective-permute-start.15 = (f32[5,8,18,1]{3,2,1,0:T(8,128)S(1)}, f32[5,8,18,1]{3,2,1,0:T(8,128)S(1)}, u32[]{:S(2)}, u32[]{:S(2)}) collective-permute-start(f32[5,8,18,1]{3,2,1,0:T(8,128)S(1)} %get-tuple-element.17), channel_id=1, source_target_pairs={{0,2},{2,4},{4,6},{6,8},{8,10},{10,12},{12,14},{14,0},{1,3},{3,5},... | collective-permute-start | bytes 8648 | tf_op jit(solution)/shard_map/ppermute | solution.py:28
  92.1 1.5 collective-permute-start.16
  92.2 1.7 collective-permute-start.17
  111.9 1.2 copy-start.6
  112.0 1.2 copy-start.7
  114.5 0.8 copy-start.4
  116.3 14.2 %all-to-all-start = ((bf16[8,32,8,128]{3,2,0,1:T(8,128)(2,1)}), bf16[8,32,8,128]{3,2,0,1:T(8,128)(2,1)S(1)}, u32[]{:S(2)}, u32[]{:S(2)}) async-start(bf16[8,32,8,128]{3,2,0,1:T(8,128)(2,1)} %copy.47), calls=%async_computation | async-start | bytes 1048576 | tf_op jit(solution)/shard_map/all_to_all | solution.py:194
  131.4 14.4 %all-to-all-start.1 = ((bf16[8,4,64,128]{3,2,1,0:T(8,128)(2,1)}), bf16[8,4,64,128]{3,2,1,0:T(8,128)(2,1)S(1)}, u32[]{:S(2)}, u32[]{:S(2)}) async-start(bf16[8,4,64,128]{3,2,1,0:T(8,128)(2,1)} %bitcast.177), calls=%async_computation.1 | async-start | bytes 1048576 | tf_op jit(solution)/shard_map/all_to_all | solution.py:193
  137.3 149.4 %all-reduce.3.cloned.1.call-start = ((), (), s32[]{:S(2)}) async-start(), calls=%async_computation.7 | async-start | bytes 524288
  147.0 4.1 copy-start.9
  149.4 151.9 %copy-start.2 = (f32[4,4,32,4,128]{4,3,2,1,0:T(4,128)S(1)}, f32[4,4,32,4,128]{4,3,2,1,0:T(4,128)}, u32[]{:S(2)}) copy-start(f32[4,4,32,4,128]{4,3,2,1,0:T(4,128)} %param.12) | copy-start | bytes 3145732
  288.9 12.2 %all-to-all-start.2 = ((f32[8,4,4,4,128]{4,2,3,1,0:T(4,128)}), f32[8,4,4,4,128]{4,2,3,1,0:T(4,128)S(1)}, u32[]{:S(2)}, u32[]{:S(2)}) async-start(f32[8,4,4,4,128]{4,2,3,1,0:T(4,128)} %stack.64), calls=%async_computation.2 | async-start | bytes 524288 | tf_op jit(solution)/shard_map/all_to_all | solution.py:19
  293.8 20.3 %reduce-scatter.2.cloned.1.call-start = ((), (), s32[]{:S(2)}) async-start(), calls=%async_computation.6 | async-start | bytes 196608 | tf_op jit(solution)/shard_map/reduce_scatter | solution.py:231
  362.0 22.1 %all-to-all-start.3 = ((f32[8,1,32768]{2,1,0:T(1,128)}), f32[8,1,32768]{2,1,0:T(1,128)S(1)}, u32[]{:S(2)}, u32[]{:S(2)}) async-start(f32[8,1,32768]{2,1,0:T(1,128)} %reshape.569), calls=%async_computation.4 | async-start | bytes 2097152 | tf_op jit(solution)/shard_map/all_to_all | solution.py:243
  440.6 16.5 %copy-start.5 = (bf16[8,32,8,128]{3,1,2,0:T(8,128)(2,1)S(1)}, bf16[8,32,8,128]{3,1,2,0:T(8,128)(2,1)}, u32[]{:S(2)}) copy-start(bf16[8,32,8,128]{3,1,2,0:T(8,128)(2,1)} %copy-done.4) | copy-start | bytes 1572868
  440.7 16.5 %copy-start.8 = (f32[32]{0:T(128)S(1)}, f32[32]{0:T(128)}, u32[]{:S(2)}) copy-start(f32[32]{0:T(128)} %param.13) | copy-start | bytes 388
Sparse Core Ops, SparseCore 0:
  151.2 135.4 all-reduce.2
  305.6 8.4 reduce-scatter.1
